TPU v7x, 32 devices: a whole 2x2x4 slice. The times are simulated.
32 devices in a mesh: groups: 2 (over x), rows: 16 (over z, y, core).
Axes of the slice: x: 2, y: 2, z: 4, core: 2. Of those that a mesh axis runs over, the one named last changes fastest.
Arguments:
- image_query: bfloat16 [12288, 2048], P(('groups', 'rows')), parts along dimension 0, may hold values from -40 to 40
- image_pairs: bfloat16 [2, 12288, 2048], P(None, ('groups', 'rows')), parts along dimension 1, may hold values from -6 to 6
- text_query: bfloat16 [512, 2048], P(('groups', 'rows')), parts along dimension 0, may hold values from -40 to 40
- text_pairs: bfloat16 [2, 512, 2048], P(None, ('groups', 'rows')), parts along dimension 1, may hold values from -6 to 6
- text_mask: int32 [512], P('groups'), parts along dimension 0, may hold values 0 or 1
- window_offsets: int32 [16, 2], replicated, may hold values from -1 to 1, as said below
- timestep: int32 [1], replicated, may hold values from 0 to 49
- gate_table: float32 [50, 2, 2048], replicated, may hold values from 0.5 to 2
Outputs:
- image_out: bfloat16 [12288, 2048], P(('groups', 'rows')), parts along dimension 0
- text_out: bfloat16 [512, 2048], P(('groups', 'rows')), parts along dimension 0
There are 2 independent parts, one for each index of `groups`. A program takes and returns all parts, laid end to end along the dimension named above; an argument that names none is the same for every part. Nothing has to cross between parts.
Inputs may be any that keep to these rules, and one draw needn't show every extreme that they name: window_offsets[h, 0] is -1 or 0 and window_offsets[h, 1] is 0 or 1; some head has -1 and some head has 1.
All inputs are finite; a program needn't handle non-finite values.
Results may differ from a plain program's by a relative error of at most 0.02.
Values may be sent and summed in bfloat16 or wider, within the bound.
A program may use at most 128 MiB of HBM per device.

v0:
```python
import math

import jax
import jax.numpy as jnp
from jax import lax
from jax.sharding import PartitionSpec as P

TILE = 384


masked_score = -1e30


def extended_2(cells, sides, width):
    for axis, dim in sides:
        count = lax.axis_size(axis)
        ends = count - 1
        head = lax.slice_in_dim(cells, 0, width, axis=dim)
        tail = lax.slice_in_dim(cells, cells.shape[dim] - width, cells.shape[dim], axis=dim)
        cells = jnp.concatenate(
            [
                lax.ppermute(tail, axis, [(i, (i + 1) % count) for i in range(ends)]),
                cells,
                lax.ppermute(head, axis, [((i + 1) % count, i) for i in range(ends)]),
            ],
            axis=dim,
        )
    return cells


def attend_tiles(queries, key_rows, value_rows, allowed, scaling):
    scores = (
        jnp.einsum("tqhe,tkhe->tqhk", queries, key_rows, preferred_element_type=jnp.float32)
        * scaling
    )
    scores = jnp.where(allowed, scores, masked_score)
    maxima = jnp.max(scores, axis=-1)
    exponent = jnp.where(allowed, jnp.exp(scores - maxima[..., None]), 0.0)
    totals = jnp.sum(exponent, axis=-1)
    summed = jnp.einsum(
        "tqhk,tkhe->tqhe",
        exponent.astype(jnp.bfloat16),
        value_rows,
        preferred_element_type=jnp.float32,
    )
    return (maxima, totals, summed.astype(jnp.bfloat16))


def attend_rows(queries, key_rows, value_rows, allowed, scaling):
    scores = (
        jnp.einsum("qhe,khe->qhk", queries, key_rows, preferred_element_type=jnp.float32) * scaling
    )
    scores = jnp.where(allowed, scores, masked_score)
    maxima = jnp.max(scores, axis=-1)
    exponent = jnp.where(allowed, jnp.exp(scores - maxima[..., None]), 0.0)
    totals = jnp.sum(exponent, axis=-1)
    summed = jnp.einsum(
        "qhk,khe->qhe",
        exponent.astype(jnp.bfloat16),
        value_rows,
        preferred_element_type=jnp.float32,
    )
    return (maxima, totals, summed.astype(jnp.bfloat16))


def combine_groups(groups):
    largest = groups[0][0]
    for member in groups[1:]:
        largest = jnp.maximum(largest, member[0])
    totals = 0.0
    summed = 0.0
    for member in groups:
        factor = jnp.exp(member[0] - largest)
        totals = totals + member[1] * factor
        summed = summed + member[2].astype(jnp.float32) * factor[..., None]
    return summed / totals[..., None]


def on_device(
    image_query,
    image_pairs,
    text_query,
    text_pairs,
    text_mask,
    window_offsets,
    timestep,
    gate_table,
):
    rows_dev, width = image_query.shape
    tiles_dev = rows_dev // TILE
    head_count = window_offsets.shape[0]
    head_width = width // head_count
    scaling = 1.0 / math.sqrt(head_width)
    position = lax.axis_index("rows")
    tiles_all = tiles_dev * lax.axis_size("rows")
    first_tile = position * tiles_dev
    reach_back = window_offsets[:, 0]
    reach_ahead = window_offsets[:, 1]
    text_queries, text_gathered = (
        lax.all_gather(text_query, "rows", axis=0, tiled=True),
        lax.all_gather(text_pairs, "rows", axis=1, tiled=True),
    )
    text_keys = text_gathered[0].reshape(-1, head_count, head_width)
    text_values = text_gathered[1].reshape(-1, head_count, head_width)
    text_allowed = (text_mask == 1)[None, None, :]
    queries = image_query.reshape(tiles_dev, TILE, head_count, head_width)
    local_keys = image_pairs[0].reshape(tiles_dev, TILE, head_count, head_width)
    local_values = image_pairs[1].reshape(tiles_dev, TILE, head_count, head_width)

    def permitted(offset):
        target = first_tile + jnp.arange(tiles_dev, dtype=jnp.int32) + offset
        inside = (target >= 0) & (target < tiles_all)
        within = (reach_back <= offset) & (offset <= reach_ahead)
        return (inside[:, None] & within[None, :])[:, None, :, None]

    flat_queries = image_query.reshape(rows_dev, head_count, head_width)
    text_group = attend_rows(flat_queries, text_keys, text_values, text_allowed, scaling)
    text_group = (
        text_group[0].reshape(tiles_dev, TILE, head_count),
        text_group[1].reshape(tiles_dev, TILE, head_count),
        text_group[2].reshape(tiles_dev, TILE, head_count, head_width),
    )
    groups = [attend_tiles(queries, local_keys, local_values, permitted(0), scaling), text_group]
    extended = extended_2(image_pairs, (("rows", 1),), TILE)
    extended = extended.reshape(2, tiles_dev + 2, TILE, head_count, head_width)
    for offset in (-1, 1):
        groups.append(
            attend_tiles(
                queries,
                extended[0, 1 + offset : 1 + offset + tiles_dev],
                extended[1, 1 + offset : 1 + offset + tiles_dev],
                permitted(offset),
                scaling,
            )
        )
    gate_rows = lax.dynamic_index_in_dim(gate_table, timestep[0], 0, keepdims=False)
    attended = combine_groups(groups).reshape(rows_dev, width)
    image_out = (attended * gate_rows[0]).astype(jnp.bfloat16)
    text_flat = text_queries.reshape(-1, head_count, head_width)
    image_keys = image_pairs[0].reshape(rows_dev, head_count, head_width)
    image_values = image_pairs[1].reshape(rows_dev, head_count, head_width)
    every_key = jnp.ones((1, 1, rows_dev), dtype=bool)
    maxima, totals, summed = attend_rows(text_flat, image_keys, image_values, every_key, scaling)
    text_dev = text_query.shape[0]
    text_start = position * text_dev
    global_max = lax.pmax(maxima, "rows")
    factor = jnp.exp(maxima - global_max)
    scaled_summed = summed.astype(jnp.float32) * factor[..., None]
    scaled_totals = totals * factor
    whole_summed, whole_totals = lax.psum((scaled_summed, scaled_totals), "rows")
    shared_summed = lax.dynamic_slice_in_dim(whole_summed, text_start, text_dev, 0)
    shared_totals = lax.dynamic_slice_in_dim(whole_totals, text_start, text_dev, 0)
    remote = (
        lax.dynamic_slice_in_dim(global_max, text_start, text_dev, 0),
        shared_totals,
        shared_summed,
    )
    own_rows = text_query.reshape(text_dev, head_count, head_width)
    own_text = attend_rows(own_rows, text_keys, text_values, text_allowed, scaling)
    text_attended = combine_groups([remote, own_text]).reshape(text_dev, width)
    text_out = (text_attended * gate_rows[1]).astype(jnp.bfloat16)
    return (image_out, text_out)


def solution(mesh):
    placed = (
        P(("groups", "rows"), None),
        P(None, ("groups", "rows"), None),
        P(("groups", "rows"), None),
        P(None, ("groups", "rows"), None),
        P("groups"),
        P(),
        P(),
        P(),
    )
    return jax.shard_map(
        on_device,
        mesh=mesh,
        in_specs=placed,
        out_specs=(P(("groups", "rows"), None), P(("groups", "rows"), None)),
        check_vma=False,
    )
```

profile of v0, /device:TPU:0, one launch (start us, length us, event | category | flops | bytes accessed | tf_op | source)
XLA Modules:
  0.0 297.9 jit_solution(4161448792035331032)
XLA Ops:
  7.2 0.0 copy-start
  7.2 0.0 all-gather.5.cloned.1.call-start
  7.2 0.7 all-gather.5.cloned.1.call-update
  7.9 0.0 all-gather.3.cloned.1.call-start
  8.0 4.0 %collective-permute-start = (bf16[2,384,2048]{2,1,0:T(8,128)(2,1)}, bf16[2,384,2048]{2,1,0:T(8,128)(2,1)}, u32[]{:S(2)}, u32[]{:S(2)}) collective-permute-start(bf16[2,384,2048]{2,1,0:T(8,128)(2,1)} %param.9), channel_id=1, source_target_pairs={{0,1},{1,2},{2,3},{3,4},{4,5},{5,6},{6,7},{7,8},{8,9},{9,10},{10,1... | collective-permute-start | bytes 9437192 | tf_op jit(solution)/shard_map/ppermute | solution.py:22
  12.0 1.3 collective-permute-start.1
  13.3 1.7 copy.59
  15.0 0.0 all-gather.3.cloned.1.call-update
  15.0 0.0 all-reduce.2.cloned.1.call-start
  15.7 0.8 constant_dynamic-slice_fusion.1
  16.5 0.8 and_bitcast_fusion.1
  17.3 4.1 %fusion.134 = (bf16[1,384,2048]{2,1,0:T(8,128)(2,1)}, bf16[1,384,2048]{2,1,0:T(8,128)(2,1)}) fusion(bf16[2,384,2048]{2,1,0:T(8,128)(2,1)} %param.9), kind=kLoop, calls=%fused_computation.155 | loop fusion | bytes 6291456 | tf_op jit(solution)/shard_map/slice | solution.py:107
  21.4 1.9 copy.95
  23.2 2.6 copy.57
  25.8 2.5 bitcast_reduce_fusion.2
  28.3 3.6 %copy-done.2 = f32[16,384,384]{2,1,0:T(8,128)} copy-done((f32[16,384,384]{2,1,0:T(8,128)}, f32[16,384,384]{2,1,0:T(8,128)S(1)}, u32[]{:S(2)}) %copy-start.2) | copy-done | bytes 9437208
  31.9 0.0 copy-done.3
  31.9 3.5 %fusion.67 = bf16[16,384,128]{1,2,0:T(8,128)(2,1)} fusion(bf16[384,16,128]{0,2,1:T(8,128)(2,1)S(1)} %bitcast.291, f32[16,384,384]{2,1,0:T(8,128)S(1)} %get-tuple-element.26, f32[384,16]{0,1:T(8,128)S(1)} %get-tuple-element.25, pred[16]{0:T(512)(128)(4,1)S(1)} %get-tuple-element.24), kind=kOutput, calls=%fused_computation.81 | convolution fusion | flops 616562688 | bytes 12607504 | tf_op jit(solution)/shard_map/tqhk,tkhe->tqhe/dot_general | solution.py:40
  35.5 28.8 %all-gather.5.cloned.1.call-done = bf16[256,2048]{1,0:T(8,128)(2,1)} async-done(((bf16[16,2048]{1,0:T(8,128)(2,1)}), bf16[256,2048]{1,0:T(8,128)(2,1)}) %all-gather.5.cloned.1.call-update) | async-done | bytes 1048592 | tf_op jit(solution)/shard_map/all_gather | solution.py:100
  64.3 2.3 copy.74
  66.7 4.9 %bitcast_reduce_fusion.3 = (f32[256,16]{0,1:T(8,128)S(1)}, f32[16,384,256]{2,1,0:T(8,128)}) fusion(bf16[384,16,128]{0,2,1:T(8,128)(2,1)S(1)} %bitcast.287, bf16[256,16,128]{0,2,1:T(8,128)(2,1)} %bitcast.294), kind=kOutput, calls=%fused_computation.23 | convolution fusion | flops 405794816 | bytes 8929280 | tf_op jit(solution)/shard_map/qhe,khe->qhk/dot_general | solution.py:51
  71.6 66.7 %pmax.7 = f32[256,16]{0,1:T(8,128)S(1)} all-reduce(f32[256,16]{0,1:T(8,128)S(1)} %get-tuple-element.35), channel_id=1, replica_groups=mesh['groups'=2,'rows'=16] {'rows'}, use_global_device_ids=true, to_apply=%region_9.10 | all-reduce | flops 4096 | bytes 32768 | tf_op jit(solution)/shard_map/pmax | solution.py:146
  138.3 4.0 %fusion.15 = f32[256,16]{0,1:T(8,128)S(1)} fusion(f32[16,384,256]{2,1,0:T(8,128)} %get-tuple-element.36, f32[256,16]{0,1:T(8,128)S(1)} %get-tuple-element.35), kind=kLoop, calls=%fused_computation.30 | loop fusion | flops 4714496 | bytes 6324224 | tf_op jit(solution)/shard_map/reduce_sum | solution.py:56
  142.3 0.6 copy-done.1
  142.9 4.4 %bitcast_multiply_fusion.2 = f32[256,16,128]{2,0,1:T(8,128)} fusion(bf16[384,16,128]{0,2,1:T(8,128)(2,1)} %bitcast.290, f32[16,384,256]{2,1,0:T(8,128)S(1)} %copy-done.1, f32[256,16]{0,1:T(8,128)S(1)} %get-tuple-element.35, f32[256,16]{0,1:T(8,128)S(1)} %get-tuple-element.6), kind=kOutput, calls=%fused_computation.79 | convolution fusion | flops 408944640 | bytes 9994240 | tf_op jit(solution)/shard_map/qhk,khe->qhe/dot_general | solution.py:57
  147.3 0.0 all-reduce.2.cloned.1.call-update
  147.3 58.2 %psum.15 = f32[256,16]{0,1:T(8,128)S(1)} all-reduce(f32[256,16]{0,1:T(8,128)S(1)} %get-tuple-element.5), channel_id=1, replica_groups=mesh['groups'=2,'rows'=16] {'rows'}, use_global_device_ids=true, to_apply=%region_13.14 | all-reduce | flops 4096 | bytes 32768 | tf_op jit(solution)/shard_map/psum | solution.py:150
  205.5 0.0 collective-permute-done
  205.5 0.0 collective-permute-done.1
  205.5 7.6 %pad_maximum_fusion = bf16[2,1152,2048]{2,1,0:T(8,128)(2,1)} fusion(bf16[2,384,2048]{2,1,0:T(8,128)(2,1)} %collective-permute-done.1, bf16[2,384,2048]{2,1,0:T(8,128)(2,1)} %param.9, bf16[2,384,2048]{2,1,0:T(8,128)(2,1)} %collective-permute-done), kind=kLoop, calls=%fused_computation | loop fusion | flops 28311552 | bytes 18874368 | tf_op jit(solution)/shard_map/concatenate | solution.py:20
  213.1 11.0 %copy.104 = bf16[288,8,16,128]{3,2,1,0:T(8,128)(2,1)} copy(bf16[288,8,16,128]{3,1,2,0:T(8,128)(2,1)} %bitcast.284) | data formatting | bytes 18874368
  224.2 5.6 %fusion.133 = (bf16[1,1,384,16,128]{4,3,2,1,0:T(8,128)(2,1)}, bf16[1,1,384,16,128]{4,3,2,1,0:T(8,128)(2,1)}, bf16[1,1,384,16,128]{4,3,2,1,0:T(8,128)(2,1)}, bf16[1,1,384,16,128]{4,3,2,1,0:T(8,128)(2,1)S(1)}) fusion(bf16[2,3,384,16,128]{4,3,2,1,0:T(8,128)(2,1)} %bitcast.285), kind=kLoop, calls=%fused_computation.154 | loop fusion | bytes 12582912 | tf_op jit(solution)/shard_map/slice | solution.py:131
  229.8 2.8 copy.99
  232.6 2.0 copy.100
  234.6 3.3 %bitcast_reduce_fusion = (f32[384,16]{0,1:T(8,128)S(1)}, f32[16,384,384]{2,1,0:T(8,128)S(1)}) fusion(pred[16]{0:T(512)(128)(4,1)S(1)} %get-tuple-element.23, bf16[1,1,384,16,128]{4,3,2,1,0:T(8,128)(2,1)} %get-tuple-element.13, bf16[384,2048]{1,0:T(8,128)(2,1)S(1)} %copy-done), kind=kOutput, calls=%fused_computation.2 | convolution fusion | flops 611051520 | bytes 12607504 | tf_op jit(solution)/shard_map/tqhe,tkhe->tqhk/dot_general | solution.py:33
  237.9 0.0 copy-start.7
  237.9 2.7 fusion.10
  240.6 0.0 slice-start
  240.6 0.0 slice-start.1
  240.6 3.5 %fusion.73 = bf16[16,128,384]{2,1,0:T(8,128)(2,1)} fusion(f32[16,384,384]{2,1,0:T(8,128)S(1)} %get-tuple-element.28, f32[384,16]{0,1:T(8,128)S(1)} %get-tuple-element.27, pred[16]{0:T(512)(128)(4,1)S(1)} %get-tuple-element.23, bf16[1,1,384,16,128]{2,4,3,1,0:T(8,128)(2,1)S(1)} %copy-done.7), kind=kOutput, calls=%fused_computation.83 | convolution fusion | flops 616562688 | bytes 12607504 | tf_op jit(solution)/shard_map/tqhk,tkhe->tqhe/dot_general | solution.py:40
  244.1 1.9 bitcast_reduce_fusion.1
  246.1 0.3 slice-done.2
  246.3 5.5 %fusion.6 = (f32[384,16]{0,1:T(8,128)S(1)}, f32[384,16]{0,1:T(8,128)S(1)}) fusion(f32[16,384,384]{2,1,0:T(8,128)S(1)} %bitcast.283, f32[384,16]{0,1:T(8,128)S(1)} %get-tuple-element.25, pred[16]{0:T(512)(128)(4,1)S(1)} %get-tuple-element.24, f32[384,16]{0,1:T(8,128)S(1)} %get-tuple-element.29, f32[16,384,384]{2,1,0:T(8,128)S(1)} %get-tuple-element.30, ...), kind=kLoop, calls=%fused_computation.16 | loop fusion | flops 23580672 | bytes 18972704 | tf_op jit(solution)/shard_map/reduce_sum | solution.py:39
  251.8 3.5 %fusion.70 = bf16[16,128,384]{2,1,0:T(8,128)(2,1)} fusion(f32[16,384,384]{2,1,0:T(8,128)S(1)} %get-tuple-element.30, f32[384,16]{0,1:T(8,128)S(1)} %get-tuple-element.29, pred[16]{0:T(512)(128)(4,1)S(1)} %get-tuple-element.22, bf16[1,1,384,16,128]{2,4,3,1,0:T(8,128)(2,1)S(1)} %copy-done.6), kind=kOutput, calls=%fused_computation.82 | convolution fusion | flops 616562688 | bytes 12607504 | tf_op jit(solution)/shard_map/tqhk,tkhe->tqhe/dot_general | solution.py:40
  255.4 6.8 %fusion.135 = (bf16[1,256,2048]{2,0,1:T(2,128)(2,1)}, bf16[1,256,2048]{2,0,1:T(2,128)(2,1)}) fusion(bf16[2,256,2048]{2,0,1:T(2,128)(2,1)} %all-gather.3.cloned.1.call-done), kind=kLoop, calls=%fused_computation.156 | loop fusion | bytes 4194304 | tf_op jit(solution)/shard_map/slice | solution.py:104
  262.2 5.8 %copy.67 = bf16[1,256,2048]{1,2,0:T(8,128)(2,1)} copy(bf16[1,256,2048]{2,0,1:T(2,128)(2,1)} %get-tuple-element.18) | data formatting | bytes 2097152 | tf_op jit(solution)/shard_map/slice | solution.py:104
  268.0 4.8 %copy.96 = bf16[1,256,2048]{1,2,0:T(8,128)(2,1)S(1)} copy(bf16[1,256,2048]{2,0,1:T(2,128)(2,1)} %get-tuple-element.19) | data formatting | bytes 2097152
  272.7 1.4 bitcast_reduce_fusion.4
  274.2 0.0 copy-start.4
  274.2 0.0 copy-start.10
  274.2 0.0 copy-start.11
  274.2 1.7 fusion.44
  276.0 0.0 copy-done.4
  276.0 0.4 copy-done.11
  276.4 0.5 copy-done.12
  276.9 4.5 %fusion.52 = f32[1,384,16,128]{1,3,2,0:T(8,128)} fusion(bf16[16,384,128]{1,2,0:T(8,128)(2,1)S(1)} %copy-done.10, bf16[16,128,384]{2,1,0:T(8,128)(2,1)S(1)} %copy-done.11, bf16[16,128,384]{2,1,0:T(8,128)(2,1)S(1)} %copy-done.12, f32[384,16]{0,1:T(8,128)S(1)} %get-tuple-element.7, f32[384,16]{0,1:T(8,128)S(1)} %get-tuple-element.11, ...), kind=kOutput, calls=%fused_computation.63 | convolution fusion | flops 420741120 | bytes 15352064 | tf_op jit(solution)/shard_map/qhk,khe->qhe/dot_general | solution.py:57
  281.4 3.6 %copy.73 = f32[384,2048]{1,0:T(8,128)} copy(f32[384,2048]{0,1:T(8,128)} %bitcast.295) | data formatting | bytes 6291456 | tf_op jit(solution)/shard_map/reshape | solution.py:137
  285.0 0.3 fusion.136
  285.3 0.2 fusion.105
  285.5 0.1 multiply_add_fusion.1
  285.6 0.0 all-reduce.2.cloned.1.call-done
  285.7 1.7 fusion.98
  287.3 0.7 fusion.108
  288.0 3.4 %multiply_convert_fusion = bf16[384,2048]{1,0:T(8,128)(2,1)} fusion(f32[384,2048]{1,0:T(8,128)} %copy.73, f32[2048]{0:T(1024)S(1)} %bitcast.296), kind=kLoop, calls=%fused_computation.72 | loop fusion | flops 1572864 | bytes 4726784 | tf_op jit(solution)/shard_map/convert_element_type | solution.py:138
  (23 shorter events, 0.1 us)
Async XLA Ops:
  7.2 18.7 %copy-start = (bf16[384,2048]{1,0:T(8,128)(2,1)S(1)}, bf16[384,2048]{1,0:T(8,128)(2,1)}, u32[]{:S(2)}) copy-start(bf16[384,2048]{1,0:T(8,128)(2,1)} %param.8) | copy-start | bytes 4718596
  7.2 57.1 %all-gather.5.cloned.1.call-start = ((), (), s32[]{:S(2)}) async-start(), calls=%async_computation.1 | async-start | bytes 1114112 | tf_op jit(solution)/shard_map/all_gather | solution.py:100
  7.9 247.5 %all-gather.3.cloned.1.call-start = ((), (), s32[]{:S(2)}) async-start(), calls=%async_computation | async-start | bytes 2228224 | tf_op jit(solution)/shard_map/all_gather | solution.py:101
  8.0 197.5 %collective-permute-start = (bf16[2,384,2048]{2,1,0:T(8,128)(2,1)}, bf16[2,384,2048]{2,1,0:T(8,128)(2,1)}, u32[]{:S(2)}, u32[]{:S(2)}) collective-permute-start(bf16[2,384,2048]{2,1,0:T(8,128)(2,1)} %param.9), channel_id=1, source_target_pairs={{0,1},{1,2},{2,3},{3,4},{4,5},{5,6},{6,7},{7,8},{8,9},{9,10},{10,1... | collective-permute-start | bytes 9437192 | tf_op jit(solution)/shard_map/ppermute | solution.py:22
  12.0 193.5 %collective-permute-start.1 = (bf16[2,384,2048]{2,1,0:T(8,128)(2,1)}, bf16[2,384,2048]{2,1,0:T(8,128)(2,1)}, u32[]{:S(2)}, u32[]{:S(2)}) collective-permute-start(bf16[2,384,2048]{2,1,0:T(8,128)(2,1)} %param.9), channel_id=1, source_target_pairs={{1,0},{2,1},{3,2},{4,3},{5,4},{6,5},{7,6},{8,7},{9,8},{10,9},{11,1... | collective-permute-start | bytes 9437192 | tf_op jit(solution)/shard_map/ppermute | solution.py:24
  15.0 270.7 %all-reduce.2.cloned.1.call-start = ((), (), s32[]{:S(2)}) async-start(), calls=%async_computation.2 | async-start | bytes 4194304 | tf_op jit(solution)/shard_map/psum | solution.py:150
  17.3 4.1 %copy-start.9 = (s32[256]{0:T(256)S(1)}, s32[256]{0:T(256)}, u32[]{:S(2)}) copy-start(s32[256]{0:T(256)} %param.12) | copy-start | bytes 3076
  25.8 6.1 %copy-start.3 = (bf16[1,384,2048]{1,2,0:T(8,128)(2,1)S(1)}, bf16[1,384,2048]{1,2,0:T(8,128)(2,1)}, u32[]{:S(2)}) copy-start(bf16[1,384,2048]{1,2,0:T(8,128)(2,1)} %copy.57) | copy-start | bytes 4718596
  28.3 3.6 %copy-start.2 = (f32[16,384,384]{2,1,0:T(8,128)}, f32[16,384,384]{2,1,0:T(8,128)S(1)}, u32[]{:S(2)}) copy-start(f32[16,384,384]{2,1,0:T(8,128)S(1)} %get-tuple-element.26) | copy-start | bytes 28311556
  138.3 4.6 %copy-start.1 = (f32[16,384,256]{2,1,0:T(8,128)S(1)}, f32[16,384,256]{2,1,0:T(8,128)}, u32[]{:S(2)}) copy-start(f32[16,384,256]{2,1,0:T(8,128)} %get-tuple-element.36) | copy-start | bytes 18874372
  237.9 2.7 copy-start.7
  240.6 3.5 %copy-start.5 = (bf16[1,1,384,16,128]{4,3,2,1,0:T(8,128)(2,1)S(1)}, bf16[1,1,384,16,128]{4,3,2,1,0:T(8,128)(2,1)}, u32[]{:S(2)}) copy-start(bf16[1,1,384,16,128]{4,3,2,1,0:T(8,128)(2,1)} %get-tuple-element.14) | copy-start | bytes 4718596
  240.6 5.4 %slice-start = ((s8[9437184]{0:T(1024)(128)(4,1)}), s8[4194304]{0:T(1024)(128)(4,1)S(1)}, s32[]{:S(2)}) async-start(s8[9437184]{0:T(1024)(128)(4,1)} %bitcast.282), calls=%async_computation.3 | async-start | bytes 8388608
  240.6 5.4 %slice-start.1 = ((s8[9437184]{0:T(1024)(128)(4,1)}), s8[1048576]{0:T(1024)(128)(4,1)S(1)}, s32[]{:S(2)}) async-start(s8[9437184]{0:T(1024)(128)(4,1)} %bitcast.282), calls=%async_computation.4 | async-start | bytes 2097152
  244.1 2.2 slice-start.2
  246.3 5.5 %copy-start.6 = (bf16[1,1,384,16,128]{2,4,3,1,0:T(8,128)(2,1)S(1)}, bf16[1,1,384,16,128]{2,4,3,1,0:T(8,128)(2,1)}, u32[]{:S(2)}) copy-start(bf16[1,1,384,16,128]{2,4,3,1,0:T(8,128)(2,1)} %copy.99) | copy-start | bytes 4718596
  274.2 1.8 copy-start.4
  274.2 1.8 copy-start.10
  274.2 2.2 copy-start.11
  274.2 2.7 copy-start.12
  281.4 3.6 %copy-start.8 = (bf16[16,2048]{1,0:T(8,128)(2,1)S(1)}, bf16[16,2048]{1,0:T(8,128)(2,1)}, u32[]{:S(2)}) copy-start(bf16[16,2048]{1,0:T(8,128)(2,1)} %param.10) | copy-start | bytes 196612
Sparse Core Ops, SparseCore 0:
  10.2 54.0 all-gather.4
  66.5 43.8 all-gather.2
  147.5 95.1 all-reduce.1
where the time goes:
time: 299 us; the launch traced here: 298 us
  blocking collectives  125 us (42%)
  local copies, waits for them, and re-layouts  61.2 us (20%)
  matrix products  35.5 us (12%)
  waiting for transfers between devices  29.6 us (10%)
  other arithmetic  26.6 us (9%)
  between operations  14.7 us (5%)
  starting transfers between devices  5.42 us (2%)
    pmax x1, blocking collectives, on_device(): global_max = lax.pmax(maxima, 'rows')  66.7 us
    psum x1, blocking collectives, on_device(): lax.psum((scaled_summed, scaled_totals), 'rows')  58.2 us
    unnamed x38, local copies, waits for them, and re-layouts  29.6 us
    all_gather x1, waiting for transfers between devices, on_device(): lax.all_gather(text_query, 'rows', axis=0, tiled=True)  28.8 us
    slice x2, local copies, waits for them, and re-layouts, on_device(): text_values = text_gathered[1].reshape(-1, head_count, head_width)  12.6 us
    dot_general x3, matrix products, attend_tiles(): jnp.einsum('tqhk,tkhe->tqhe', exponent.astype(jnp.bfloat16), value_rows,...  10.6 us
    dot_general x3, matrix products, attend_rows(): jnp.einsum('qhk,khe->qhe', exponent.astype(jnp.bfloat16), value_rows, pre...  10.5 us
    reduce_sum x2, other arithmetic, attend_tiles(): totals = jnp.sum(exponent, axis=-1)  8.14 us
  transfers between devices with their start and end apart: 5, of which 1 were waited for; matrix products, arithmetic and copies ran while one was open for 38% of the time, Pallas kernels for 0%

commit v1 on v0

--- a/solution.py
+++ b/solution.py
@@ -1,8 +1,11 @@
+import functools
 import math
 
 import jax
 import jax.numpy as jnp
 from jax import lax
+from jax.experimental import pallas as pl
+from jax.experimental.pallas import tpu as pltpu
 from jax.sharding import PartitionSpec as P
 
 TILE = 384
@@ -162,6 +165,449 @@
     return (image_out, text_out)
 
 
+CAPS = (11,)
+MESH = pl.DeviceIdType.MESH
+
+
+def flipped(pos, bits):
+    out = pos
+    bit = 1
+    while bit <= bits:
+        if bits & bit:
+            out = out + bit - 2 * bit * ((pos // bit) % 2)
+        bit *= 2
+    return out
+
+
+def stage_bits(count):
+    bits = []
+    bit = count // 2
+    while bit >= 1:
+        bits.append(bit)
+        bit //= 2
+    if len(bits) == 4:
+        bits = [bits[0], bits[2], bits[1], bits[3]]
+    return bits
+
+
+def joint_kernel(
+    count,
+    slots,
+    heads,
+    scale2,
+    table,
+    q_ref,
+    pairs_ref,
+    tq_ref,
+    tp_ref,
+    bias_ref,
+    gate_ref,
+    out_ref,
+    tout_ref,
+    hq,
+    hkv,
+    packed,
+    landed,
+    tq_all,
+    tkv_all,
+    part_o,
+    part_ml,
+    stat,
+    o_send,
+    o_recv,
+    s_send,
+    s_recv,
+    gs_sem,
+    gr_sem,
+    hs_sem,
+    hr_sem,
+    as_sem,
+    ar_sem,
+):
+    pos = lax.axis_index("rows")
+    grp = lax.axis_index("groups")
+    rows = q_ref.shape[0]
+    tdev = tq_ref.shape[0]
+    text = count * tdev
+    width = q_ref.shape[1] // heads
+
+    barrier = pltpu.get_barrier_semaphore()
+
+    def greet(d, _):
+        pl.semaphore_signal(
+            barrier, inc=1, device_id=(grp, lax.rem(pos + d, count)), device_id_type=MESH
+        )
+        return 0
+
+    lax.fori_loop(1, count, greet, 0)
+    pl.semaphore_wait(barrier, count - 1)
+
+    def cols(h):
+        return pl.ds(pl.multiple_of(h * width, width), width)
+
+    bits = stage_bits(count)
+    refs = (tq_all, tkv_all)
+
+    def gather_copy(kind, number, block, partner):
+        ref = tq_all.at[block] if kind == 0 else tkv_all.at[:, block]
+        return pltpu.make_async_remote_copy(
+            src_ref=ref,
+            dst_ref=ref,
+            send_sem=gs_sem.at[kind, number],
+            recv_sem=gr_sem.at[kind, number],
+            device_id=(grp, partner),
+            device_id_type=MESH,
+        )
+
+    plan = []
+    offsets = [0]
+    number = 0
+    for bit in bits:
+        stage = []
+        for off in offsets:
+            stage.append((number, off, bit))
+            number += 1
+        plan.append(stage)
+        offsets = offsets + [off ^ bit for off in offsets]
+
+    def gather_start(kind, stage):
+        for num, off, bit in plan[stage]:
+            gather_copy(kind, num, flipped(pos, off), flipped(pos, bit)).start()
+
+    def gather_land(kind, stage):
+        for num, off, bit in plan[stage]:
+            gather_copy(kind, num, flipped(pos, off ^ bit), flipped(pos, bit)).wait_recv()
+
+    def gather_sent(kind, stage):
+        for num, off, bit in plan[stage]:
+            gather_copy(kind, num, flipped(pos, off), flipped(pos, bit)).wait_send()
+
+    tq_all[pos] = tq_ref[...]
+    tkv_all[:, pos] = tp_ref[...]
+    gather_start(0, 0)
+    gather_start(1, 0)
+
+    def halo_copy(side, j):
+        partner = pos + 1 if side == 0 else pos - 1
+        return pltpu.make_async_remote_copy(
+            src_ref=packed.at[side, j],
+            dst_ref=landed.at[side, j],
+            send_sem=hs_sem.at[side, j],
+            recv_sem=hr_sem.at[side, j],
+            device_id=(grp, partner),
+            device_id_type=MESH,
+        )
+
+    has_prev = pos > 0
+    has_next = pos < count - 1
+
+    for h in range(heads):
+        at = slice(h * width, (h + 1) * width)
+        hkv[h] = pairs_ref[:, :, at]
+        hq[h] = q_ref[:, at]
+
+    def pack(j, _):
+        @pl.when(has_next)
+        def _():
+            h = table[0, j]
+            packed[0, j] = hkv[h]
+            halo_copy(0, j).start()
+
+        @pl.when(has_prev)
+        def _():
+            h = table[1, j]
+            packed[1, j] = hkv[h]
+            halo_copy(1, j).start()
+
+        return 0
+
+    lax.fori_loop(0, slots, pack, 0)
+
+    def partial(keys, values, queries, bias):
+        scores = lax.dot_general(
+            keys, queries, (((1,), (1,)), ((), ())), preferred_element_type=jnp.float32
+        )
+        if bias is not None:
+            scores = scores + bias
+        top = jnp.max(scores, axis=0, keepdims=True)
+        weights = jnp.exp2((scores - top) * scale2)
+        total = jnp.sum(weights, axis=0, keepdims=True)
+        summed = lax.dot_general(
+            values,
+            weights.astype(jnp.bfloat16),
+            (((0,), (0,)), ((), ())),
+            preferred_element_type=jnp.float32,
+        )
+        return top, total, summed
+
+    def keep(kind, j, result):
+        top, total, summed = result
+        part_o[kind, j] = summed
+        part_ml[kind, j, 0:1, :] = top
+        part_ml[kind, j, 1:2, :] = total
+
+    def local_head(h, _):
+        keep(
+            0,
+            h,
+            partial(hkv[h, 0], hkv[h, 1], hq[h], None),
+        )
+        return 0
+
+    stages = len(bits)
+    done = 0
+    for stage in range(stages):
+        upto = heads * (stage + 1) // stages
+        lax.fori_loop(done, upto, local_head, 0)
+        done = upto
+        for kind in (0, 1):
+            gather_land(kind, stage)
+            if stage + 1 < stages:
+                gather_start(kind, stage + 1)
+
+    stat[...] = jnp.zeros_like(stat)
+    own_bias = bias_ref[pl.ds(pl.multiple_of(pos * tdev, tdev), tdev), 0:1]
+    slab_bias = jnp.concatenate([jnp.zeros((rows, 1), jnp.float32), own_bias], axis=0)
+
+    def text_head(h, _):
+        keys = jnp.concatenate([hkv[h, 0], tp_ref[0, :, cols(h)]], axis=0)
+        values = jnp.concatenate([hkv[h, 1], tp_ref[1, :, cols(h)]], axis=0)
+        queries = tq_all[:, :, cols(h)].reshape(text, width)
+        top, total, summed = partial(keys, values, queries, slab_bias)
+        stat[0, pl.ds(h, 1), :] = top
+        stat[1, pl.ds(h, 1), :] = total
+        o_send[:, :, cols(h)] = summed.T.astype(jnp.bfloat16).reshape(count, tdev, width)
+        return 0
+
+    lax.fori_loop(0, heads, text_head, 0)
+    s_send[:, 0] = stat[0].T.reshape(count, tdev, 128)
+    s_send[:, 1] = stat[1].T.reshape(count, tdev, 128)
+
+    def spread_copy(kind, d, source, target):
+        send, recv = ((o_send, o_recv), (s_send, s_recv))[kind]
+        return pltpu.make_async_remote_copy(
+            src_ref=send.at[target],
+            dst_ref=recv.at[source],
+            send_sem=as_sem.at[kind, d],
+            recv_sem=ar_sem.at[kind, d],
+            device_id=(grp, target),
+            device_id_type=MESH,
+        )
+
+    def spread_start(d, _):
+        target = lax.rem(pos + d, count)
+        spread_copy(0, d, pos, target).start()
+        spread_copy(1, d, pos, target).start()
+        return 0
+
+    lax.fori_loop(1, count, spread_start, 0)
+    o_recv[pos] = o_send[pos]
+    s_recv[pos] = s_send[pos]
+
+    def image_text(h, _):
+        keys = tkv_all[0, :, :, cols(h)].reshape(text, width)
+        values = tkv_all[1, :, :, cols(h)].reshape(text, width)
+        keep(1, h, partial(keys, values, hq[h], bias_ref[:, 0:1]))
+        return 0
+
+    lax.fori_loop(0, heads, image_text, 0)
+
+    def halo_head(j, _):
+        @pl.when(has_prev)
+        def _():
+            halo_copy(0, j).wait_recv()
+            queries = hq[table[0, j]]
+            keep(2, j, partial(landed[0, j, 0], landed[0, j, 1], queries, None))
+
+        @pl.when(has_next)
+        def _():
+            halo_copy(1, j).wait_recv()
+            queries = hq[table[1, j]]
+            keep(3, j, partial(landed[1, j, 0], landed[1, j, 1], queries, None))
+
+        return 0
+
+    lax.fori_loop(0, slots, halo_head, 0)
+
+    prev_i = jnp.where(has_prev, 1, 0)
+    next_i = jnp.where(has_next, 1, 0)
+
+    def finish(h, _):
+        slot_p, slot_n = table[2, h], table[3, h]
+        use_p = jnp.full((1, rows), table[4, h] * prev_i, jnp.int32) == 1
+        use_n = jnp.full((1, rows), table[5, h] * next_i, jnp.int32) == 1
+        m0, l0 = part_ml[0, h, 0:1, :], part_ml[0, h, 1:2, :]
+        m1, l1 = part_ml[1, h, 0:1, :], part_ml[1, h, 1:2, :]
+        ml_p, ml_n = part_ml[2, slot_p], part_ml[3, slot_n]
+        m2 = jnp.where(use_p, ml_p[0:1], masked_score)
+        m3 = jnp.where(use_n, ml_n[0:1], masked_score)
+        l2 = jnp.where(use_p, ml_p[1:2], 0.0)
+        l3 = jnp.where(use_n, ml_n[1:2], 0.0)
+        top = jnp.maximum(jnp.maximum(m0, m1), jnp.maximum(m2, m3))
+        f0 = jnp.exp2((m0 - top) * scale2)
+        f1 = jnp.exp2((m1 - top) * scale2)
+        f2 = jnp.exp2((m2 - top) * scale2)
+        f3 = jnp.exp2((m3 - top) * scale2)
+        total = l0 * f0 + l1 * f1 + l2 * f2 + l3 * f3
+        share = 1.0 / total
+        summed = (
+            part_o[0, h] * (f0 * share)
+            + part_o[1, h] * (f1 * share)
+            + jnp.where(use_p, part_o[2, slot_p], 0.0) * (f2 * share)
+            + jnp.where(use_n, part_o[3, slot_n], 0.0) * (f3 * share)
+        )
+        out_ref[:, cols(h)] = (summed.T * gate_ref[0:1, cols(h)]).astype(jnp.bfloat16)
+        return 0
+
+    lax.fori_loop(0, heads, finish, 0)
+
+    def spread_land(d, _):
+        source = lax.rem(pos + count - d, count)
+        for kind in (0, 1):
+            recv = (o_recv, s_recv)[kind]
+            send = (o_send, s_send)[kind]
+            pltpu.make_async_remote_copy(
+                src_ref=send.at[source],
+                dst_ref=recv.at[source],
+                send_sem=as_sem.at[kind, d],
+                recv_sem=ar_sem.at[kind, d],
+                device_id=(grp, source),
+                device_id_type=MESH,
+            ).wait_recv()
+        return 0
+
+    lax.fori_loop(1, count, spread_land, 0)
+    tops = s_recv[:, 0]
+    top = jnp.max(tops, axis=0, keepdims=True)
+    factors = jnp.exp2((tops - top) * scale2)
+    total = jnp.sum(s_recv[:, 1] * factors, axis=0)
+    factors = factors / jnp.where(total == 0.0, 1.0, total)[None]
+    for h in range(heads):
+        acc = jnp.zeros((tdev, width), jnp.float32)
+        for d in range(count):
+            acc = acc + o_recv[d, :, h * width : (h + 1) * width].astype(jnp.float32) * factors[
+                d, :, h : h + 1
+            ]
+        gate = gate_ref[1:2, h * width : (h + 1) * width]
+        tout_ref[:, h * width : (h + 1) * width] = (acc * gate).astype(jnp.bfloat16)
+
+    for stage in range(stages):
+        gather_sent(0, stage)
+        gather_sent(1, stage)
+
+    def spread_sent(d, _):
+        target = lax.rem(pos + d, count)
+        spread_copy(0, d, pos, target).wait_send()
+        spread_copy(1, d, pos, target).wait_send()
+        return 0
+
+    lax.fori_loop(1, count, spread_sent, 0)
+
+    def halo_sent(j, _):
+        @pl.when(has_next)
+        def _():
+            halo_copy(0, j).wait_send()
+
+        @pl.when(has_prev)
+        def _():
+            halo_copy(1, j).wait_send()
+
+        return 0
+
+    lax.fori_loop(0, slots, halo_sent, 0)
+
+
+def head_table(window_offsets):
+    heads = window_offsets.shape[0]
+    flags = jnp.stack([window_offsets[:, 0] == -1, window_offsets[:, 1] == 1]).astype(jnp.int32)
+    index = jnp.arange(heads, dtype=jnp.int32)
+    before = (index[:, None] < index[None, :]).astype(jnp.int32)
+    ranks = jnp.sum(flags[:, :, None] * before[None], axis=1)
+    hit = (ranks[:, None, :] == index[None, :, None]).astype(jnp.int32) * flags[:, None, :]
+    lists = jnp.sum(hit * index[None, None, :], axis=2)
+    return jnp.concatenate([lists, ranks * flags, flags], axis=0), jnp.max(jnp.sum(flags, axis=1))
+
+
+def fused_device(
+    image_query,
+    image_pairs,
+    text_query,
+    text_pairs,
+    text_mask,
+    window_offsets,
+    timestep,
+    gate_table,
+):
+    rows, width_all = image_query.shape
+    heads = window_offsets.shape[0]
+    width = width_all // heads
+    count = lax.axis_size("rows")
+    tdev = text_query.shape[0]
+    text = tdev * count
+    table, most = head_table(window_offsets)
+    bias = jnp.broadcast_to(
+        jnp.where(text_mask == 1, 0.0, masked_score).astype(jnp.float32)[:, None], (text, 128)
+    )
+    gate = lax.dynamic_index_in_dim(gate_table, timestep[0], 0, keepdims=False)
+    scale2 = math.log2(math.e) / math.sqrt(width)
+    vmem = pl.BlockSpec(memory_space=pltpu.VMEM)
+    bf16, f32 = jnp.bfloat16, jnp.float32
+
+    def build(slots, ident):
+        return pl.pallas_call(
+            functools.partial(joint_kernel, count, slots, heads, scale2),
+            out_shape=(
+                jax.ShapeDtypeStruct(image_query.shape, bf16),
+                jax.ShapeDtypeStruct(text_query.shape, bf16),
+            ),
+            in_specs=[pl.BlockSpec(memory_space=pltpu.SMEM)] + [vmem] * 6,
+            out_specs=(vmem, vmem),
+            scratch_shapes=[
+                pltpu.VMEM((heads, rows, width), bf16),
+                pltpu.VMEM((heads, 2, rows, width), bf16),
+                pltpu.VMEM((2, slots, 2, rows, width), bf16),
+                pltpu.VMEM((2, slots, 2, rows, width), bf16),
+                pltpu.VMEM((count, tdev, width_all), bf16),
+                pltpu.VMEM((2, count, tdev, width_all), bf16),
+                pltpu.VMEM((4, heads, width, rows), f32),
+                pltpu.VMEM((4, heads, 8, rows), f32),
+                pltpu.VMEM((2, 128, text), f32),
+                pltpu.VMEM((count, tdev, width_all), bf16),
+                pltpu.VMEM((count, tdev, width_all), bf16),
+                pltpu.VMEM((count, 2, tdev, 128), f32),
+                pltpu.VMEM((count, 2, tdev, 128), f32),
+                pltpu.SemaphoreType.DMA((2, count)),
+                pltpu.SemaphoreType.DMA((2, count)),
+                pltpu.SemaphoreType.DMA((2, slots)),
+                pltpu.SemaphoreType.DMA((2, slots)),
+                pltpu.SemaphoreType.DMA((2, count)),
+                pltpu.SemaphoreType.DMA((2, count)),
+            ],
+            compiler_params=pltpu.CompilerParams(
+                collective_id=ident, has_side_effects=True, vmem_limit_bytes=56 << 20
+            ),
+        )
+
+    args = (table, image_query, image_pairs, text_query, text_pairs, bias, gate)
+    sizes = [cap for cap in CAPS if cap < heads] + [heads]
+    branches = [build(slots, i) for i, slots in enumerate(sizes)]
+    if len(branches) == 1:
+        return branches[0](*args)
+    which = sum((most > cap).astype(jnp.int32) for cap in sizes[:-1])
+    return lax.switch(which, branches, *args)
+
+
+def joint(*args):
+    rows = args[0].shape[0]
+    tdev = args[2].shape[0]
+    heads = args[5].shape[0]
+    count = lax.axis_size("rows")
+    fits = rows == TILE and tdev % 16 == 0 and count & (count - 1) == 0 and heads <= 128
+    if fits and count <= 32 and args[0].shape[1] == heads * 128:
+        return fused_device(*args)
+    return on_device(*args)
+
+
 def solution(mesh):
     placed = (
         P(("groups", "rows"), None),
@@ -174,7 +620,7 @@
         P(),
     )
     return jax.shard_map(
-        on_device,
+        joint,
         mesh=mesh,
         in_specs=placed,
         out_specs=(P(("groups", "rows"), None), P(("groups", "rows"), None)),

time: 299 us -> 126 us (0.42)
  the two profiles are of different devices: /device:TPU:0 before, /device:TPU:15 now
where the time goes in v1:
time: 126 us
  Pallas kernels  116 us (92%)
  local copies, waits for them, and re-layouts  3.85 us (3%)
  other arithmetic  2.43 us (2%)
  loops' own time  1.96 us (2%)
  between operations  1.31 us (1%)
    pallas_call x1, Pallas kernels, fused_device(): return lax.switch(which, branches, *args)  116 us

profile of v1, /device:TPU:15, one launch (start us, length us, event | category | flops | bytes accessed | tf_op | source)
XLA Modules:
  0.0 125.6 jit_solution(12369677361035269562)
XLA Ops:
  0.6 0.8 compare_bitcast_fusion.1
  1.4 0.1 multiply_reduce_fusion.1
  1.5 0.1 broadcast_select_fusion
  1.6 0.1 multiply_reduce_fusion
  1.7 0.6 reduce_max.9
  3.0 120.8 %conditional.1 = ((bf16[384,2048]{1,0:T(8,128)(2,1)S(1)}, bf16[16,2048]{1,0:T(8,128)(2,1)S(1)})) conditional(s32[]{:T(128)} %clamp.3, (s32[6,16]{1,0:T(8,128)S(1)}, bf16[384,2048]{1,0:T(8,128)(2,1)}, bf16[2,384,2048]{2,1,0:T(8,128)(2,1)}, bf16[16,2048]{1,0:T(8,128)(2,1)}, bf16[2,16,2048]{2,1,0:T(8,128)(2,1)}, /*index=5*/s32[256]{0:T(256)}, ...), branch_computations={%region_4.5_spmd.clone, %region_5.6_spmd.clone} | conditional | flops 515 | bytes 166962 | solution.py:597
  5.0 0.7 compare_select_fusion
  5.7 1.3 %dynamic-slice_bitcast_fusion.gate_ref = f32[2,2048]{1,0:T(2,128)} fusion(f32[50,2,2048]{2,1,0:T(2,128)} %get-tuple-element.124, s32[]{:T(128)S(6)} %select_n.15), kind=kLoop, calls=%fused_computation | loop fusion | bytes 32772 | tf_op jit(solution)/shard_map/jit(dynamic_index_in_dim)/squeeze | solution.py:551
  7.0 0.8 broadcast_in_dim.31.bias_ref
  7.8 116.1 %branch_0_fun.1 = (bf16[384,2048]{1,0:T(8,128)(2,1)S(1)}, bf16[16,2048]{1,0:T(8,128)(2,1)S(1)}) custom-call(s32[6,16]{1,0:T(8,128)S(1)} %get-tuple-element.114.table, bf16[384,2048]{1,0:T(8,128)(2,1)} %get-tuple-element.117.q_ref, bf16[2,384,2048]{2,1,0:T(8,128)(2,1)} %get-tuple-element.118.pairs_ref, bf16[16,2048]{1,0:T(8,128)(2,1)} %get-tuple-element.119.tq_ref, ...), custom_call_target="tpu_custom_call" | custom-call | tf_op jit(solution)/shard_map/cond/branch_0_fun/pallas_call | solution.py:597
  123.8 1.1 copy.48
  125.0 0.6 copy.49
  (3 shorter events, 0.0 us)

commit v2 on v1

--- a/solution.py
+++ b/solution.py
@@ -165,7 +165,8 @@
     return (image_out, text_out)
 
 
-CAPS = (11,)
+CAPS = (10, 12)
+LEAD = 2
 MESH = pl.DeviceIdType.MESH
 
 
@@ -188,6 +189,11 @@
     if len(bits) == 4:
         bits = [bits[0], bits[2], bits[1], bits[3]]
     return bits
+
+
+def fold_bits(count):
+    bits = stage_bits(count)
+    return bits[::-1]
 
 
 def joint_kernel(
@@ -321,7 +327,6 @@
 
         return 0
 
-    lax.fori_loop(0, slots, pack, 0)
 
     def partial(keys, values, queries, bias):
         scores = lax.dot_general(
@@ -346,88 +351,140 @@
         part_ml[kind, j, 0:1, :] = top
         part_ml[kind, j, 1:2, :] = total
 
-    def local_head(h, _):
-        keep(
-            0,
-            h,
-            partial(hkv[h, 0], hkv[h, 1], hq[h], None),
-        )
-        return 0
+    def pairwise(first, last, head):
+        def two(i, _):
+            h = first + 2 * i
+            results = (head(h), head(h + 1))
+            for k in range(2):
+                for kind, j, result in results[k]:
+                    keep(kind, j, result)
+            return 0
+
+        lax.fori_loop(0, (last - first) // 2, two, 0)
+
+    def local_head(h):
+        return [(0, h, partial(hkv[h, 0], hkv[h, 1], hq[h], None))]
 
     stages = len(bits)
-    done = 0
+    done, begun = 0, 0
     for stage in range(stages):
+        ahead = min(slots, LEAD * (stage + 1))
+        lax.fori_loop(begun, ahead, pack, 0)
+        begun = ahead
         upto = heads * (stage + 1) // stages
-        lax.fori_loop(done, upto, local_head, 0)
+        pairwise(done, upto, local_head)
         done = upto
         for kind in (0, 1):
             gather_land(kind, stage)
             if stage + 1 < stages:
                 gather_start(kind, stage + 1)
+    lax.fori_loop(begun, slots, pack, 0)
 
     stat[...] = jnp.zeros_like(stat)
     own_bias = bias_ref[pl.ds(pl.multiple_of(pos * tdev, tdev), tdev), 0:1]
     slab_bias = jnp.concatenate([jnp.zeros((rows, 1), jnp.float32), own_bias], axis=0)
 
-    def text_head(h, _):
+    def text_head(h):
         keys = jnp.concatenate([hkv[h, 0], tp_ref[0, :, cols(h)]], axis=0)
         values = jnp.concatenate([hkv[h, 1], tp_ref[1, :, cols(h)]], axis=0)
         queries = tq_all[:, :, cols(h)].reshape(text, width)
-        top, total, summed = partial(keys, values, queries, slab_bias)
-        stat[0, pl.ds(h, 1), :] = top
-        stat[1, pl.ds(h, 1), :] = total
-        o_send[:, :, cols(h)] = summed.T.astype(jnp.bfloat16).reshape(count, tdev, width)
+        return partial(keys, values, queries, slab_bias)
+
+    def text_pair(i, _):
+        results = (text_head(2 * i), text_head(2 * i + 1))
+        for k in range(2):
+            h = 2 * i + k
+            top, total, summed = results[k]
+            stat[0, pl.ds(h, 1), :] = top
+            stat[1, pl.ds(h, 1), :] = total
+            o_send[:, :, cols(h)] = summed.T.astype(jnp.bfloat16).reshape(count, tdev, width)
         return 0
 
-    lax.fori_loop(0, heads, text_head, 0)
+    lax.fori_loop(0, heads // 2, text_pair, 0)
     s_send[:, 0] = stat[0].T.reshape(count, tdev, 128)
     s_send[:, 1] = stat[1].T.reshape(count, tdev, 128)
 
-    def spread_copy(kind, d, source, target):
+    halving = fold_bits(count)
+    folds = []
+    number = 0
+    for k in range(len(halving)):
+        spans = [0]
+        for bit in halving[k + 1 :]:
+            spans = spans + [off ^ bit for off in spans]
+        folds.append([(number + i, off, halving[k]) for i, off in enumerate(spans)])
+        number += len(spans)
+
+    def fold_copy(kind, num, off, bit):
         send, recv = ((o_send, o_recv), (s_send, s_recv))[kind]
         return pltpu.make_async_remote_copy(
-            src_ref=send.at[target],
-            dst_ref=recv.at[source],
-            send_sem=as_sem.at[kind, d],
-            recv_sem=ar_sem.at[kind, d],
-            device_id=(grp, target),
+            src_ref=send.at[flipped(pos, off ^ bit)],
+            dst_ref=recv.at[num],
+            send_sem=as_sem.at[kind, num],
+            recv_sem=ar_sem.at[kind, num],
+            device_id=(grp, flipped(pos, bit)),
             device_id_type=MESH,
         )
 
-    def spread_start(d, _):
-        target = lax.rem(pos + d, count)
-        spread_copy(0, d, pos, target).start()
-        spread_copy(1, d, pos, target).start()
-        return 0
-
-    lax.fori_loop(1, count, spread_start, 0)
-    o_recv[pos] = o_send[pos]
-    s_recv[pos] = s_send[pos]
-
-    def image_text(h, _):
+    def fold_start(k):
+        for num, off, bit in folds[k]:
+            fold_copy(0, num, off, bit).start()
+            fold_copy(1, num, off, bit).start()
+
+    def fold_merge(k):
+        for num, off, bit in folds[k]:
+            fold_copy(0, num, off, bit).wait_recv()
+            fold_copy(1, num, off, bit).wait_recv()
+            block = flipped(pos, off)
+            m0, m1 = s_send[block, 0], s_recv[num, 0]
+            top = jnp.maximum(m0, m1)
+            f0 = jnp.exp2((m0 - top) * scale2)
+            f1 = jnp.exp2((m1 - top) * scale2)
+            s_send[block, 0] = top
+            s_send[block, 1] = s_send[block, 1] * f0 + s_recv[num, 1] * f1
+            for h in range(heads):
+                at = slice(h * width, (h + 1) * width)
+                o_send[block, :, at] = (
+                    o_send[block, :, at].astype(jnp.float32) * f0[:, h : h + 1]
+                    + o_recv[num, :, at].astype(jnp.float32) * f1[:, h : h + 1]
+                ).astype(jnp.bfloat16)
+
+    fold_start(0)
+
+    def image_text(h):
         keys = tkv_all[0, :, :, cols(h)].reshape(text, width)
         values = tkv_all[1, :, :, cols(h)].reshape(text, width)
-        keep(1, h, partial(keys, values, hq[h], bias_ref[:, 0:1]))
-        return 0
-
-    lax.fori_loop(0, heads, image_text, 0)
+        return [(1, h, partial(keys, values, hq[h], bias_ref[:, 0:1]))]
 
     def halo_head(j, _):
         @pl.when(has_prev)
         def _():
             halo_copy(0, j).wait_recv()
-            queries = hq[table[0, j]]
-            keep(2, j, partial(landed[0, j, 0], landed[0, j, 1], queries, None))
 
         @pl.when(has_next)
         def _():
             halo_copy(1, j).wait_recv()
-            queries = hq[table[1, j]]
-            keep(3, j, partial(landed[1, j, 0], landed[1, j, 1], queries, None))
-
+
+        before = partial(landed[0, j, 0], landed[0, j, 1], hq[table[0, j]], None)
+        after = partial(landed[1, j, 0], landed[1, j, 1], hq[table[1, j]], None)
+        keep(2, j, before)
+        keep(3, j, after)
         return 0
 
-    lax.fori_loop(0, slots, halo_head, 0)
+    last = len(folds)
+    done, seen = 0, 0
+    for k in range(last):
+        if k < last // 2:
+            upto = heads * (k + 1) // (last // 2)
+            pairwise(done, upto, image_text)
+            done = upto
+        else:
+            upto = slots * (k + 1 - last // 2) // (last - last // 2 + 1)
+            lax.fori_loop(seen, upto, halo_head, 0)
+            seen = upto
+        fold_merge(k)
+        if k + 1 < last:
+            fold_start(k + 1)
+    lax.fori_loop(seen, slots, halo_head, 0)
 
     prev_i = jnp.where(has_prev, 1, 0)
     next_i = jnp.where(has_next, 1, 0)
@@ -461,47 +518,20 @@
 
     lax.fori_loop(0, heads, finish, 0)
 
-    def spread_land(d, _):
-        source = lax.rem(pos + count - d, count)
-        for kind in (0, 1):
-            recv = (o_recv, s_recv)[kind]
-            send = (o_send, s_send)[kind]
-            pltpu.make_async_remote_copy(
-                src_ref=send.at[source],
-                dst_ref=recv.at[source],
-                send_sem=as_sem.at[kind, d],
-                recv_sem=ar_sem.at[kind, d],
-                device_id=(grp, source),
-                device_id_type=MESH,
-            ).wait_recv()
-        return 0
-
-    lax.fori_loop(1, count, spread_land, 0)
-    tops = s_recv[:, 0]
-    top = jnp.max(tops, axis=0, keepdims=True)
-    factors = jnp.exp2((tops - top) * scale2)
-    total = jnp.sum(s_recv[:, 1] * factors, axis=0)
-    factors = factors / jnp.where(total == 0.0, 1.0, total)[None]
+    share = 1.0 / s_send[pos, 1]
     for h in range(heads):
-        acc = jnp.zeros((tdev, width), jnp.float32)
-        for d in range(count):
-            acc = acc + o_recv[d, :, h * width : (h + 1) * width].astype(jnp.float32) * factors[
-                d, :, h : h + 1
-            ]
-        gate = gate_ref[1:2, h * width : (h + 1) * width]
-        tout_ref[:, h * width : (h + 1) * width] = (acc * gate).astype(jnp.bfloat16)
+        at = slice(h * width, (h + 1) * width)
+        rescaled = o_send[pos, :, at].astype(jnp.float32) * share[:, h : h + 1]
+        tout_ref[:, at] = (rescaled * gate_ref[1:2, at]).astype(jnp.bfloat16)
 
     for stage in range(stages):
         gather_sent(0, stage)
         gather_sent(1, stage)
 
-    def spread_sent(d, _):
-        target = lax.rem(pos + d, count)
-        spread_copy(0, d, pos, target).wait_send()
-        spread_copy(1, d, pos, target).wait_send()
-        return 0
-
-    lax.fori_loop(1, count, spread_sent, 0)
+    for stage in folds:
+        for num, off, bit in stage:
+            fold_copy(0, num, off, bit).wait_send()
+            fold_copy(1, num, off, bit).wait_send()
 
     def halo_sent(j, _):
         @pl.when(has_next)

time: 126 us -> 98.8 us (0.78)
  the two profiles are of different devices: /device:TPU:15 before, /device:TPU:0 now
where the time goes in v2:
time: 98.8 us; the launch traced here: 97.2 us
  Pallas kernels  86.7 us (88%)
  local copies, waits for them, and re-layouts  3.85 us (4%)
  other arithmetic  2.43 us (2%)
  loops' own time  2.18 us (2%)
  between operations  1.96 us (2%)
    pallas_call x1, Pallas kernels, fused_device(): return lax.switch(which, branches, *args)  86.7 us
    another operation x1, loops' own time, fused_device(): return lax.switch(which, branches, *args)  2.18 us

profile of v2, /device:TPU:0, one launch (start us, length us, event | category | flops | bytes accessed | tf_op | source)
XLA Modules:
  0.0 97.2 jit_solution(5405401436383054)
XLA Ops:
  0.6 0.8 compare_bitcast_fusion.1
  1.4 0.1 multiply_reduce_fusion.1
  1.5 0.1 broadcast_select_fusion
  1.6 0.1 multiply_reduce_fusion
  1.7 0.6 reduce_max.9
  3.7 91.7 %conditional.1 = ((bf16[384,2048]{1,0:T(8,128)(2,1)S(1)}, bf16[16,2048]{1,0:T(8,128)(2,1)S(1)})) conditional(s32[]{:T(128)} %clamp.3, (s32[6,16]{1,0:T(8,128)S(1)}, bf16[384,2048]{1,0:T(8,128)(2,1)}, bf16[2,384,2048]{2,1,0:T(8,128)(2,1)}, bf16[16,2048]{1,0:T(8,128)(2,1)}, bf16[2,16,2048]{2,1,0:T(8,128)(2,1)}, ...), branch_computations={%region_4.5_spmd.clone, %region_5.6_spmd.clone, %region_6.7_spmd.c... | conditional | flops 515 | bytes 166962 | solution.py:627
  5.7 0.7 compare_select_fusion
  6.3 1.3 %dynamic-slice_bitcast_fusion.gate_ref = f32[2,2048]{1,0:T(2,128)} fusion(f32[50,2,2048]{2,1,0:T(2,128)} %get-tuple-element.179, s32[]{:T(128)S(6)} %select_n.17), kind=kLoop, calls=%fused_computation | loop fusion | bytes 32772 | tf_op jit(solution)/shard_map/jit(dynamic_index_in_dim)/squeeze | solution.py:581
  7.7 0.8 broadcast_in_dim.34.bias_ref
  8.4 86.7 %branch_0_fun.1 = (bf16[384,2048]{1,0:T(8,128)(2,1)S(1)}, bf16[16,2048]{1,0:T(8,128)(2,1)S(1)}) custom-call(s32[6,16]{1,0:T(8,128)S(1)} %get-tuple-element.169.table, bf16[384,2048]{1,0:T(8,128)(2,1)} %get-tuple-element.172.q_ref, bf16[2,384,2048]{2,1,0:T(8,128)(2,1)} %get-tuple-element.173.pairs_ref, bf16[16,2048]{1,0:T(8,128)(2,1)} %get-tuple-element.174.tq_ref, ...), custom_call_target="tpu_custom_call" | custom-call | tf_op jit(solution)/shard_map/cond/branch_0_fun/pallas_call | solution.py:627
  95.4 1.1 %copy.66 = bf16[384,2048]{1,0:T(8,128)(2,1)} copy(bf16[384,2048]{1,0:T(8,128)(2,1)S(1)} %get-tuple-element.262) | data formatting | bytes 3145728
  96.5 0.6 copy.67
  (3 shorter events, 0.0 us)
